TPU v7x, 32 devices: a whole 2x2x4 slice. The times are simulated.
32 devices in a mesh: tile: 8 (over z, x), depth: 4 (over y, core).
Axes of the slice: x: 2, y: 2, z: 4, core: 2. Of those that a mesh axis runs over, the one named last changes fastest.
Arguments:
- phase: float32 [64, 512, 256], P('tile', 'depth'), may hold values from -1 to 1
- solute: float32 [64, 512, 256], P('tile', 'depth'), may hold values from -3 to 3
- dphase: float32 [64, 512, 256], P('tile', 'depth'), may hold values from -6 to 6
- dsolute: float32 [64, 512, 256], P('tile', 'depth'), may hold values from -6 to 6
- labels: int32 [64, 256], P('tile'), may hold values from 0 to 3
- pixel_mask: int32 [64, 256], P('tile'), may hold values 0 or 1
Outputs:
- hess_phase: float32 [64, 512, 256], P('tile', 'depth')
- hess_solute: float32 [64, 512, 256], P('tile', 'depth')
- change: float32 [64, 256], P('tile')
All inputs are finite; a program needn't handle non-finite values. No bound on the sum of `pixel_mask` on one device may be relied on, other than what follows from the above.
Results may differ from a plain program's by a relative error of at most 0.00002.
Values sent between devices are 32-bit elements; how exact they have to be, the bound alone decides.
A program may use at most 64 MiB of HBM per device.

v0:
```python
import math

import jax
import jax.numpy as jnp
from jax import lax
from jax.sharding import PartitionSpec as P

step_size = 0.1
rejection = 0.5


def extended(cells, sides, width):
    for axis, dim in sides:
        count = lax.axis_size(axis)
        ends = count - 1
        head = lax.slice_in_dim(cells, 0, width, axis=dim)
        tail = lax.slice_in_dim(cells, cells.shape[dim] - width, cells.shape[dim], axis=dim)
        cells = jnp.concatenate(
            [
                lax.ppermute(tail, axis, [(i, (i + 1) % count) for i in range(ends)]),
                cells,
                lax.ppermute(head, axis, [((i + 1) % count, i) for i in range(ends)]),
            ],
            axis=dim,
        )
    return cells


def lap_inner(padded):
    core = padded[..., 1:-1, 1:-1, :]
    zero_col = jnp.zeros_like(core[..., :1])
    total = padded[..., 2:, 1:-1, :] + padded[..., :-2, 1:-1, :]
    total = total + padded[..., 1:-1, 2:, :] + padded[..., 1:-1, :-2, :]
    total = total + jnp.concatenate([core[..., 1:], zero_col], axis=-1)
    total = total + jnp.concatenate([zero_col, core[..., :-1]], axis=-1)
    return total - 6.0 * core


def growth(labels):
    return jnp.where(
        labels == 0, 0.6, jnp.where(labels == 1, 1.0, jnp.where(labels == 2, 1.7, 0.8))
    ).astype(jnp.float32)


def slopes(phase, solute, grow):
    shell = 1.0 - phase * phase
    return (grow * (1.0 - 3.0 * phase * phase) + 4.0 * phase * shell * solute, -shell * shell)


def advance(padded, grow):
    beside_all = lap_inner(padded)
    center = padded[:, 1:-1, 1:-1, :]
    phase, solute, dphase, dsolute = (center[0], center[1], center[2], center[3])
    slope_phase, slope_solute = slopes(phase, solute, grow)
    shell = 1.0 - phase * phase
    phase_next = phase + step_size * (
        beside_all[0] + grow * (phase - phase * phase * phase) - shell * shell * solute
    )
    solute_next = solute + step_size * beside_all[1] + rejection * (phase_next - phase)
    dphase_next = dphase + step_size * (
        beside_all[2] + slope_phase * dphase + slope_solute * dsolute
    )
    dsolute_next = dsolute + step_size * beside_all[3] + rejection * (dphase_next - dphase)
    return (
        jnp.stack([phase_next, solute_next, dphase_next, dsolute_next]),
        slope_phase,
        slope_solute,
    )


def retreat(padded, slope_phase, slope_solute):
    beside_all = lap_inner(padded)
    center = padded[:, 1:-1, 1:-1, :]
    carried, adj_solute = (center[0], center[1])
    adj_phase = (
        carried + step_size * (beside_all[0] + slope_phase * carried) - rejection * adj_solute
    )
    adj_next = adj_solute + step_size * beside_all[1] + step_size * slope_solute * carried
    return (adj_phase, adj_next)


def local(phase, solute, dphase, dsolute, labels, pixel_mask):
    rows_here, layers, cols_all = phase.shape
    slabs = lax.axis_size("depth")
    grow_plain = growth(labels)
    state = jnp.stack([phase, solute, dphase, dsolute])
    saved = []
    for section in range(2):
        padded = extended(state, (("tile", 1), ("depth", 2)), 1)
        state, slope_phase, slope_solute = advance(padded, grow_plain[:, None, :])
        saved.append((slope_phase, slope_solute))
    totals, shifts = lax.psum((jnp.sum(state[1], axis=1), jnp.sum(state[3], axis=1)), "depth")
    depth_root = math.sqrt(layers * slabs)
    bright = jnp.exp(-totals / depth_root)
    change = -bright * shifts / depth_root
    backdrop = -bright * pixel_mask.astype(jnp.float32) * change
    adj_solute = jnp.broadcast_to(backdrop[:, None, :], phase.shape)
    paired = jnp.stack([rejection * adj_solute, adj_solute])
    for section in (1, 0):
        padded = extended(paired, (("tile", 1), ("depth", 2)), 1)
        adj_phase, adj_solute = retreat(padded, saved[section][0], saved[section][1])
        paired = jnp.stack([adj_phase + rejection * adj_solute, adj_solute])
    return (adj_phase, adj_solute, change)


def solution(mesh):
    placed = (
        P("tile", "depth", None),
        P("tile", "depth", None),
        P("tile", "depth", None),
        P("tile", "depth", None),
        P("tile", None),
        P("tile", None),
    )
    return jax.shard_map(
        local,
        mesh=mesh,
        in_specs=placed,
        out_specs=(P("tile", "depth", None), P("tile", "depth", None), P("tile", None)),
        check_vma=False,
    )
```

profile of v0, /device:TPU:0, one launch (start us, length us, event | category | flops | bytes accessed | tf_op | source)
XLA Modules:
  0.0 155.9 jit_solution(14813809208919900493)
XLA Ops:
  0.6 2.5 %pad_maximum_fusion.41 = f32[4,8,128,256]{3,2,1,0:T(8,128)S(1)} fusion(f32[1,8,128,256]{3,2,1,0:T(8,128)} %bitcast.125, f32[1,8,128,256]{3,2,1,0:T(8,128)} %bitcast.122, f32[1,8,128,256]{3,2,1,0:T(8,128)} %bitcast.128, f32[1,8,128,256]{3,2,1,0:T(8,128)} %bitcast.131), kind=kLoop, calls=%fused_computation.61 | loop fusion | flops 3145728 | bytes 8388608 | tf_op jit(solution)/shard_map/stack | solution.py:86
  3.1 0.1 fusion.94
  3.2 1.3 collective-permute-start
  4.5 0.0 copy-start
  4.5 0.0 copy-start.1
  4.5 0.0 copy-start.2
  4.5 0.0 copy-start.3
  4.5 5.8 %collective-permute-start.1 = (f32[4,1,128,256]{3,2,1,0:T(8,128)S(1)}, f32[4,1,128,256]{3,2,1,0:T(8,128)S(1)}, u32[]{:S(2)}, u32[]{:S(2)}) collective-permute-start(f32[4,1,128,256]{3,2,1,0:T(8,128)S(1)} %get-tuple-element.30), channel_id=1, source_target_pairs={{0,4},{4,8},{8,12},{12,16},{16,20},{20,24},{24,28},{1,5},{5,9},{9,... | collective-permute-start | bytes 1572872 | tf_op jit(solution)/shard_map/ppermute | solution.py:20
  10.3 1.5 fusion.93
  11.8 0.0 copy-start.5
  11.8 8.1 %collective-permute-done = f32[4,1,128,256]{3,2,1,0:T(8,128)S(1)} collective-permute-done((f32[4,1,128,256]{3,2,1,0:T(8,128)S(1)}, f32[4,1,128,256]{3,2,1,0:T(8,128)S(1)}, u32[]{:S(2)}, u32[]{:S(2)}) %collective-permute-start) | collective-permute-done | bytes 524320 | tf_op jit(solution)/shard_map/ppermute | solution.py:22
  19.9 11.4 %collective-permute-done.1 = f32[4,1,128,256]{3,2,1,0:T(8,128)S(1)} collective-permute-done((f32[4,1,128,256]{3,2,1,0:T(8,128)S(1)}, f32[4,1,128,256]{3,2,1,0:T(8,128)S(1)}, u32[]{:S(2)}, u32[]{:S(2)}) %collective-permute-start.1) | collective-permute-done | bytes 524320 | tf_op jit(solution)/shard_map/ppermute | solution.py:20
  31.3 0.0 copy-done
  31.3 0.0 copy-done.3
  31.3 0.1 pad_maximum_fusion.79
  31.4 1.3 collective-permute-start.2
  32.7 3.0 %collective-permute-start.3 = (f32[4,10,1,256]{3,2,1,0:T(1,128)S(1)}, f32[4,10,1,256]{3,2,1,0:T(1,128)S(1)}, u32[]{:S(2)}, u32[]{:S(2)}) collective-permute-start(f32[4,10,1,256]{3,2,1,0:T(1,128)S(1)} %get-tuple-element.23), channel_id=1, source_target_pairs={{0,1},{1,2},{2,3},{4,5},{5,6},{6,7},{8,9},{9,10},{10,11},{12,13},{... | collective-permute-start | bytes 122888 | tf_op jit(solution)/shard_map/ppermute | solution.py:20
  35.7 0.0 copy-done.5
  35.8 0.0 collective-permute-done.2
  35.8 0.8 collective-permute-done.3
  36.6 5.8 %fusion.9 = f32[4,8,128,256]{3,2,1,0:T(8,128)S(1)} fusion(f32[4,10,1,256]{3,2,1,0:T(1,128)S(1)} %collective-permute-done.3, f32[4,1,128,256]{3,2,1,0:T(8,128)S(1)} %collective-permute-done, f32[4,1,128,256]{3,2,1,0:T(8,128)S(1)} %collective-permute-done.1, f32[1,8,128,256]{3,2,1,0:T(8,128)S(1)} %bitcast.127, f32[1,8,128,256]{3,2,1,0:T(8,128)S(1)} %bitcast.124, ...), kind=kLoop, calls=%fused_computation.39 | loop fusion | flops 31457280 | bytes 17874944 | tf_op jit(solution)/shard_map/sub | solution.py:36
  42.4 1.3 fusion.87
  43.7 0.4 pad_maximum_fusion.42
  44.0 0.1 fusion.92
  44.1 1.3 collective-permute-start.4
  45.4 5.1 %collective-permute-start.5 = (f32[4,1,128,256]{3,2,1,0:T(8,128)S(1)}, f32[4,1,128,256]{3,2,1,0:T(8,128)S(1)}, u32[]{:S(2)}, u32[]{:S(2)}) collective-permute-start(f32[4,1,128,256]{3,2,1,0:T(8,128)S(1)} %get-tuple-element.26), channel_id=1, source_target_pairs={{0,4},{4,8},{8,12},{12,16},{16,20},{20,24},{24,28},{1,5},{5,9},{9,... | collective-permute-start | bytes 1572872 | tf_op jit(solution)/shard_map/ppermute | solution.py:20
  50.5 10.0 %collective-permute-done.4 = f32[4,1,128,256]{3,2,1,0:T(8,128)S(1)} collective-permute-done((f32[4,1,128,256]{3,2,1,0:T(8,128)S(1)}, f32[4,1,128,256]{3,2,1,0:T(8,128)S(1)}, u32[]{:S(2)}, u32[]{:S(2)}) %collective-permute-start.4) | collective-permute-done | bytes 524320 | tf_op jit(solution)/shard_map/ppermute | solution.py:22
  60.5 12.4 %collective-permute-done.5 = f32[4,1,128,256]{3,2,1,0:T(8,128)S(1)} collective-permute-done((f32[4,1,128,256]{3,2,1,0:T(8,128)S(1)}, f32[4,1,128,256]{3,2,1,0:T(8,128)S(1)}, u32[]{:S(2)}, u32[]{:S(2)}) %collective-permute-start.5) | collective-permute-done | bytes 524320 | tf_op jit(solution)/shard_map/ppermute | solution.py:20
  72.9 0.1 pad_maximum_fusion.73
  73.0 1.3 collective-permute-start.6
  74.3 3.0 %collective-permute-start.7 = (f32[4,10,1,256]{3,2,1,0:T(1,128)S(1)}, f32[4,10,1,256]{3,2,1,0:T(1,128)S(1)}, u32[]{:S(2)}, u32[]{:S(2)}) collective-permute-start(f32[4,10,1,256]{3,2,1,0:T(1,128)S(1)} %get-tuple-element.21), channel_id=1, source_target_pairs={{0,1},{1,2},{2,3},{4,5},{5,6},{6,7},{8,9},{9,10},{10,11},{12,13},{... | collective-permute-start | bytes 122888 | tf_op jit(solution)/shard_map/ppermute | solution.py:20
  77.3 3.5 %fusion.91 = (f32[4,8,128,255]{3,2,1,0:T(8,128)S(1)}, f32[4,8,128,255]{3,2,1,0:T(8,128)}) fusion(f32[4,8,128,256]{3,2,1,0:T(8,128)S(1)} %pad_maximum_fusion.42), kind=kLoop, calls=%fused_computation.220 | loop fusion | bytes 16711680 | tf_op jit(solution)/shard_map/slice | solution.py:34
  80.8 0.0 collective-permute-done.6
  80.8 0.0 collective-permute-done.7
  80.8 9.4 %fusion.3 = f32[4,8,128,256]{3,2,1,0:T(8,128)S(1)} fusion(f32[4,10,1,256]{3,2,1,0:T(1,128)S(1)} %collective-permute-done.7, f32[4,1,128,256]{3,2,1,0:T(8,128)S(1)} %collective-permute-done.4, f32[4,1,128,256]{3,2,1,0:T(8,128)S(1)} %collective-permute-done.5, f32[1,8,128,256]{3,2,1,0:T(8,128)S(1)} %get-tuple-element.12, f32[1,8,128,256]{3,2,1,0:T(8,128)S(1)} %bitcast.136, ...), kind=kLoop, calls=%fused_computation.13 | loop fusion | flops 31457280 | bytes 17874944 | tf_op jit(solution)/shard_map/sub | solution.py:36
  90.3 0.0 copy-start.6
  90.3 1.6 %fusion.82 = (f32[8,256]{1,0:T(8,128)S(1)}, f32[8,256]{1,0:T(8,128)S(1)}) fusion(f32[8,128,256]{2,1,0:T(8,128)S(1)} %get-tuple-element.17, f32[8,128,256]{2,1,0:T(8,128)S(1)} %get-tuple-element.16, f32[4,8,128,256]{3,2,1,0:T(8,128)S(1)} %fusion.3, f32[8,256]{1,0:T(8,128)S(1)} %select_select_fusion, f32[8,128,256]{2,1,0:T(8,128)S(1)} %get-tuple-element.13, ...), kind=kLoop, calls=%fused_computation.188 | loop fusion | flops 11530240 | bytes 10510336 | tf_op jit(solution)/shard_map/reduce_sum | solution.py:92
  91.8 11.4 %all-reduce.8 = (f32[8,256]{1,0:T(8,128)S(1)}, f32[8,256]{1,0:T(8,128)S(1)}) all-reduce(f32[8,256]{1,0:T(8,128)S(1)} %get-tuple-element.4, f32[8,256]{1,0:T(8,128)S(1)} %get-tuple-element.3), channel_id=1, replica_groups=mesh['tile'=8,'depth'=4] {'depth'}, use_global_device_ids=true, to_apply=%region_3.4 | all-reduce | flops 4096 | bytes 32768 | tf_op jit(solution)/shard_map/psum | solution.py:92
  103.3 0.0 copy-done.6
  103.3 0.6 broadcast_multiply_fusion
  103.9 0.1 stack.55
  104.0 0.1 stack_broadcast_in_dim.2
  104.1 1.3 collective-permute-start.8
  105.4 4.9 %collective-permute-start.9 = (f32[2,1,128,256]{3,2,1,0:T(8,128)S(1)}, f32[2,1,128,256]{3,2,1,0:T(8,128)S(1)}, u32[]{:S(2)}, u32[]{:S(2)}) collective-permute-start(f32[2,1,128,256]{3,2,1,0:T(8,128)S(1)} %get-tuple-element.42), channel_id=1, source_target_pairs={{0,4},{4,8},{8,12},{12,16},{16,20},{20,24},{24,28},{1,5},{5,9},{9,... | collective-permute-start | bytes 786440 | tf_op jit(solution)/shard_map/ppermute | solution.py:20
  110.4 4.0 %collective-permute-done.8 = f32[2,1,128,256]{3,2,1,0:T(8,128)S(1)} collective-permute-done((f32[2,1,128,256]{3,2,1,0:T(8,128)S(1)}, f32[2,1,128,256]{3,2,1,0:T(8,128)S(1)}, u32[]{:S(2)}, u32[]{:S(2)}) %collective-permute-start.8) | collective-permute-done | bytes 262176 | tf_op jit(solution)/shard_map/ppermute | solution.py:22
  114.3 5.8 %collective-permute-done.9 = f32[2,1,128,256]{3,2,1,0:T(8,128)S(1)} collective-permute-done((f32[2,1,128,256]{3,2,1,0:T(8,128)S(1)}, f32[2,1,128,256]{3,2,1,0:T(8,128)S(1)}, u32[]{:S(2)}, u32[]{:S(2)}) %collective-permute-start.9) | collective-permute-done | bytes 262176 | tf_op jit(solution)/shard_map/ppermute | solution.py:20
  120.1 1.3 collective-permute-start.10
  121.4 3.2 %collective-permute-start.11 = (f32[2,10,1,256]{3,2,1,0:T(1,128)S(1)}, f32[2,10,1,256]{3,2,1,0:T(1,128)S(1)}, u32[]{:S(2)}, u32[]{:S(2)}) collective-permute-start(f32[2,10,1,256]{3,2,1,0:T(1,128)S(1)} %get-tuple-element.35), channel_id=1, source_target_pairs={{0,1},{1,2},{2,3},{4,5},{5,6},{6,7},{8,9},{9,10},{10,11},{12,13},{... | collective-permute-start | bytes 61448 | tf_op jit(solution)/shard_map/ppermute | solution.py:20
  124.7 0.7 fusion.16
  125.4 0.0 collective-permute-done.10
  125.4 0.0 collective-permute-done.11
  125.4 2.4 %fusion.19 = f32[2,8,128,256]{3,2,1,0:T(8,128)S(1)} fusion(f32[1,8,128,256]{3,2,1,0:T(8,128)S(1)} %stack_broadcast_in_dim.2, f32[1,8,128,256]{3,2,1,0:T(8,128)S(1)} %stack.55, f32[2,10,1,256]{3,2,1,0:T(1,128)S(1)} %collective-permute-done.11, f32[2,1,128,256]{3,2,1,0:T(8,128)S(1)} %collective-permute-done.8, ...), kind=kLoop, calls=%fused_computation.79 | loop fusion | flops 10485760 | bytes 8937472 | tf_op jit(solution)/shard_map/sub | solution.py:36
  127.8 0.8 fusion.64
  128.7 1.3 collective-permute-start.12
  130.0 5.0 %collective-permute-start.13 = (f32[2,1,128,256]{3,2,1,0:T(8,128)S(1)}, f32[2,1,128,256]{3,2,1,0:T(8,128)S(1)}, u32[]{:S(2)}, u32[]{:S(2)}) collective-permute-start(f32[2,1,128,256]{3,2,1,0:T(8,128)S(1)} %get-tuple-element.38), channel_id=1, source_target_pairs={{0,4},{4,8},{8,12},{12,16},{16,20},{20,24},{24,28},{1,5},{5,9},{9,... | collective-permute-start | bytes 786440 | tf_op jit(solution)/shard_map/ppermute | solution.py:20
  135.0 4.7 %collective-permute-done.12 = f32[2,1,128,256]{3,2,1,0:T(8,128)S(1)} collective-permute-done((f32[2,1,128,256]{3,2,1,0:T(8,128)S(1)}, f32[2,1,128,256]{3,2,1,0:T(8,128)S(1)}, u32[]{:S(2)}, u32[]{:S(2)}) %collective-permute-start.12) | collective-permute-done | bytes 262176 | tf_op jit(solution)/shard_map/ppermute | solution.py:22
  139.7 6.5 %collective-permute-done.13 = f32[2,1,128,256]{3,2,1,0:T(8,128)S(1)} collective-permute-done((f32[2,1,128,256]{3,2,1,0:T(8,128)S(1)}, f32[2,1,128,256]{3,2,1,0:T(8,128)S(1)}, u32[]{:S(2)}, u32[]{:S(2)}) %collective-permute-start.13) | collective-permute-done | bytes 262176 | tf_op jit(solution)/shard_map/ppermute | solution.py:20
  146.3 1.3 collective-permute-start.14
  147.6 3.0 %collective-permute-start.15 = (f32[2,10,1,256]{3,2,1,0:T(1,128)S(1)}, f32[2,10,1,256]{3,2,1,0:T(1,128)S(1)}, u32[]{:S(2)}, u32[]{:S(2)}) collective-permute-start(f32[2,10,1,256]{3,2,1,0:T(1,128)S(1)} %get-tuple-element.33), channel_id=1, source_target_pairs={{0,1},{1,2},{2,3},{4,5},{5,6},{6,7},{8,9},{9,10},{10,11},{12,13},{... | collective-permute-start | bytes 61448 | tf_op jit(solution)/shard_map/ppermute | solution.py:20
  150.6 0.7 fusion.12
  151.4 0.0 collective-permute-done.14
  151.4 0.1 collective-permute-done.15
  151.5 2.3 %fusion.15 = f32[2,8,128,256]{3,2,1,0:T(8,128)S(1)} fusion(f32[1,8,128,256]{3,2,1,0:T(8,128)S(1)} %bitcast.115, f32[1,8,128,256]{3,2,1,0:T(8,128)S(1)} %bitcast.111, f32[2,10,1,256]{3,2,1,0:T(1,128)S(1)} %collective-permute-done.15, f32[2,1,128,256]{3,2,1,0:T(8,128)S(1)} %collective-permute-done.12, f32[2,1,128,256]{3,2,1,0:T(8,128)S(1)} %collective-permute-done.13, ...), kind=kLoop, calls=%fused_computation.75 | loop fusion | flops 10485760 | bytes 8937472 | tf_op jit(solution)/shard_map/sub | solution.py:36
  153.8 2.1 %fusion.52 = (f32[8,128,256]{2,1,0:T(8,128)}, f32[8,128,256]{2,1,0:T(8,128)}) fusion(f32[8,128,256]{2,1,0:T(8,128)S(1)} %get-tuple-element.8, f32[2,8,128,256]{3,2,1,0:T(8,128)S(1)} %fusion.15, f32[8,128,256]{2,1,0:T(8,128)S(1)} %get-tuple-element.7, f32[8,128,256]{2,1,0:T(8,128)S(1)} %copy-done.4, f32[8,128,256]{2,1,0:T(8,128)S(1)} %copy-done.2, ...), kind=kLoop, calls=%fused_computation.147 | loop fusion | flops 6029312 | bytes 8396800 | tf_op jit(solution)/shard_map/add | solution.py:78
  (10 shorter events, 0.1 us)
Async XLA Ops:
  3.2 16.8 %collective-permute-start = (f32[4,1,128,256]{3,2,1,0:T(8,128)S(1)}, f32[4,1,128,256]{3,2,1,0:T(8,128)S(1)}, u32[]{:S(2)}, u32[]{:S(2)}) collective-permute-start(f32[4,1,128,256]{3,2,1,0:T(8,128)S(1)} %get-tuple-element.31), channel_id=1, source_target_pairs={{4,0},{8,4},{12,8},{16,12},{20,16},{24,20},{28,24},{5,1},{9,5},{13... | collective-permute-start | bytes 1572872 | tf_op jit(solution)/shard_map/ppermute | solution.py:22
  4.5 26.9 %copy-start = (f32[8,128,256]{2,1,0:T(8,128)S(1)}, f32[8,128,256]{2,1,0:T(8,128)}, u32[]{:S(2)}) copy-start(f32[8,128,256]{2,1,0:T(8,128)} %param.8) | copy-start | bytes 3145732
  4.5 26.8 %copy-start.1 = (f32[8,128,256]{2,1,0:T(8,128)S(1)}, f32[8,128,256]{2,1,0:T(8,128)}, u32[]{:S(2)}) copy-start(f32[8,128,256]{2,1,0:T(8,128)} %param.9) | copy-start | bytes 3145732
  4.5 26.8 %copy-start.2 = (f32[8,128,256]{2,1,0:T(8,128)S(1)}, f32[8,128,256]{2,1,0:T(8,128)}, u32[]{:S(2)}) copy-start(f32[8,128,256]{2,1,0:T(8,128)} %param.7) | copy-start | bytes 3145732
  4.5 26.8 %copy-start.3 = (f32[8,128,256]{2,1,0:T(8,128)S(1)}, f32[8,128,256]{2,1,0:T(8,128)}, u32[]{:S(2)}) copy-start(f32[8,128,256]{2,1,0:T(8,128)} %param.6) | copy-start | bytes 3145732
  4.5 26.8 %collective-permute-start.1 = (f32[4,1,128,256]{3,2,1,0:T(8,128)S(1)}, f32[4,1,128,256]{3,2,1,0:T(8,128)S(1)}, u32[]{:S(2)}, u32[]{:S(2)}) collective-permute-start(f32[4,1,128,256]{3,2,1,0:T(8,128)S(1)} %get-tuple-element.30), channel_id=1, source_target_pairs={{0,4},{4,8},{8,12},{12,16},{16,20},{20,24},{24,28},{1,5},{5,9},{9,... | collective-permute-start | bytes 1572872 | tf_op jit(solution)/shard_map/ppermute | solution.py:20
  11.8 23.9 %copy-start.5 = (s32[8,256]{1,0:T(8,128)S(1)}, s32[8,256]{1,0:T(8,128)}, u32[]{:S(2)}) copy-start(s32[8,256]{1,0:T(8,128)} %param.10) | copy-start | bytes 24580
  31.4 4.4 %collective-permute-start.2 = (f32[4,10,1,256]{3,2,1,0:T(1,128)S(1)}, f32[4,10,1,256]{3,2,1,0:T(1,128)S(1)}, u32[]{:S(2)}, u32[]{:S(2)}) collective-permute-start(f32[4,10,1,256]{3,2,1,0:T(1,128)S(1)} %get-tuple-element.22), channel_id=1, source_target_pairs={{1,0},{2,1},{3,2},{5,4},{6,5},{7,6},{9,8},{10,9},{11,10},{13,12},{... | collective-permute-start | bytes 122888 | tf_op jit(solution)/shard_map/ppermute | solution.py:22
  32.7 3.9 %collective-permute-start.3 = (f32[4,10,1,256]{3,2,1,0:T(1,128)S(1)}, f32[4,10,1,256]{3,2,1,0:T(1,128)S(1)}, u32[]{:S(2)}, u32[]{:S(2)}) collective-permute-start(f32[4,10,1,256]{3,2,1,0:T(1,128)S(1)} %get-tuple-element.23), channel_id=1, source_target_pairs={{0,1},{1,2},{2,3},{4,5},{5,6},{6,7},{8,9},{9,10},{10,11},{12,13},{... | collective-permute-start | bytes 122888 | tf_op jit(solution)/shard_map/ppermute | solution.py:20
  44.1 16.4 %collective-permute-start.4 = (f32[4,1,128,256]{3,2,1,0:T(8,128)S(1)}, f32[4,1,128,256]{3,2,1,0:T(8,128)S(1)}, u32[]{:S(2)}, u32[]{:S(2)}) collective-permute-start(f32[4,1,128,256]{3,2,1,0:T(8,128)S(1)} %get-tuple-element.27), channel_id=1, source_target_pairs={{4,0},{8,4},{12,8},{16,12},{20,16},{24,20},{28,24},{5,1},{9,5},{13... | collective-permute-start | bytes 1572872 | tf_op jit(solution)/shard_map/ppermute | solution.py:22
  45.4 27.5 %collective-permute-start.5 = (f32[4,1,128,256]{3,2,1,0:T(8,128)S(1)}, f32[4,1,128,256]{3,2,1,0:T(8,128)S(1)}, u32[]{:S(2)}, u32[]{:S(2)}) collective-permute-start(f32[4,1,128,256]{3,2,1,0:T(8,128)S(1)} %get-tuple-element.26), channel_id=1, source_target_pairs={{0,4},{4,8},{8,12},{12,16},{16,20},{20,24},{24,28},{1,5},{5,9},{9,... | collective-permute-start | bytes 1572872 | tf_op jit(solution)/shard_map/ppermute | solution.py:20
  73.0 7.9 %collective-permute-start.6 = (f32[4,10,1,256]{3,2,1,0:T(1,128)S(1)}, f32[4,10,1,256]{3,2,1,0:T(1,128)S(1)}, u32[]{:S(2)}, u32[]{:S(2)}) collective-permute-start(f32[4,10,1,256]{3,2,1,0:T(1,128)S(1)} %get-tuple-element.20), channel_id=1, source_target_pairs={{1,0},{2,1},{3,2},{5,4},{6,5},{7,6},{9,8},{10,9},{11,10},{13,12},{... | collective-permute-start | bytes 122888 | tf_op jit(solution)/shard_map/ppermute | solution.py:22
  74.3 6.6 %collective-permute-start.7 = (f32[4,10,1,256]{3,2,1,0:T(1,128)S(1)}, f32[4,10,1,256]{3,2,1,0:T(1,128)S(1)}, u32[]{:S(2)}, u32[]{:S(2)}) collective-permute-start(f32[4,10,1,256]{3,2,1,0:T(1,128)S(1)} %get-tuple-element.21), channel_id=1, source_target_pairs={{0,1},{1,2},{2,3},{4,5},{5,6},{6,7},{8,9},{9,10},{10,11},{12,13},{... | collective-permute-start | bytes 122888 | tf_op jit(solution)/shard_map/ppermute | solution.py:20
  90.3 13.0 %copy-start.6 = (s32[8,256]{1,0:T(8,128)S(1)}, s32[8,256]{1,0:T(8,128)}, u32[]{:S(2)}) copy-start(s32[8,256]{1,0:T(8,128)} %param.11) | copy-start | bytes 24580
  104.1 10.2 %collective-permute-start.8 = (f32[2,1,128,256]{3,2,1,0:T(8,128)S(1)}, f32[2,1,128,256]{3,2,1,0:T(8,128)S(1)}, u32[]{:S(2)}, u32[]{:S(2)}) collective-permute-start(f32[2,1,128,256]{3,2,1,0:T(8,128)S(1)} %get-tuple-element.43), channel_id=1, source_target_pairs={{4,0},{8,4},{12,8},{16,12},{20,16},{24,20},{28,24},{5,1},{9,5},{13... | collective-permute-start | bytes 786440 | tf_op jit(solution)/shard_map/ppermute | solution.py:22
  105.4 14.7 %collective-permute-start.9 = (f32[2,1,128,256]{3,2,1,0:T(8,128)S(1)}, f32[2,1,128,256]{3,2,1,0:T(8,128)S(1)}, u32[]{:S(2)}, u32[]{:S(2)}) collective-permute-start(f32[2,1,128,256]{3,2,1,0:T(8,128)S(1)} %get-tuple-element.42), channel_id=1, source_target_pairs={{0,4},{4,8},{8,12},{12,16},{16,20},{20,24},{24,28},{1,5},{5,9},{9,... | collective-permute-start | bytes 786440 | tf_op jit(solution)/shard_map/ppermute | solution.py:20
  120.1 5.3 %collective-permute-start.10 = (f32[2,10,1,256]{3,2,1,0:T(1,128)S(1)}, f32[2,10,1,256]{3,2,1,0:T(1,128)S(1)}, u32[]{:S(2)}, u32[]{:S(2)}) collective-permute-start(f32[2,10,1,256]{3,2,1,0:T(1,128)S(1)} %get-tuple-element.34), channel_id=1, source_target_pairs={{1,0},{2,1},{3,2},{5,4},{6,5},{7,6},{9,8},{10,9},{11,10},{13,12},{... | collective-permute-start | bytes 61448 | tf_op jit(solution)/shard_map/ppermute | solution.py:22
  121.4 4.0 %collective-permute-start.11 = (f32[2,10,1,256]{3,2,1,0:T(1,128)S(1)}, f32[2,10,1,256]{3,2,1,0:T(1,128)S(1)}, u32[]{:S(2)}, u32[]{:S(2)}) collective-permute-start(f32[2,10,1,256]{3,2,1,0:T(1,128)S(1)} %get-tuple-element.35), channel_id=1, source_target_pairs={{0,1},{1,2},{2,3},{4,5},{5,6},{6,7},{8,9},{9,10},{10,11},{12,13},{... | collective-permute-start | bytes 61448 | tf_op jit(solution)/shard_map/ppermute | solution.py:20
  128.7 11.0 %collective-permute-start.12 = (f32[2,1,128,256]{3,2,1,0:T(8,128)S(1)}, f32[2,1,128,256]{3,2,1,0:T(8,128)S(1)}, u32[]{:S(2)}, u32[]{:S(2)}) collective-permute-start(f32[2,1,128,256]{3,2,1,0:T(8,128)S(1)} %get-tuple-element.39), channel_id=1, source_target_pairs={{4,0},{8,4},{12,8},{16,12},{20,16},{24,20},{28,24},{5,1},{9,5},{13... | collective-permute-start | bytes 786440 | tf_op jit(solution)/shard_map/ppermute | solution.py:22
  130.0 16.3 %collective-permute-start.13 = (f32[2,1,128,256]{3,2,1,0:T(8,128)S(1)}, f32[2,1,128,256]{3,2,1,0:T(8,128)S(1)}, u32[]{:S(2)}, u32[]{:S(2)}) collective-permute-start(f32[2,1,128,256]{3,2,1,0:T(8,128)S(1)} %get-tuple-element.38), channel_id=1, source_target_pairs={{0,4},{4,8},{8,12},{12,16},{16,20},{20,24},{24,28},{1,5},{5,9},{9,... | collective-permute-start | bytes 786440 | tf_op jit(solution)/shard_map/ppermute | solution.py:20
  146.3 5.1 %collective-permute-start.14 = (f32[2,10,1,256]{3,2,1,0:T(1,128)S(1)}, f32[2,10,1,256]{3,2,1,0:T(1,128)S(1)}, u32[]{:S(2)}, u32[]{:S(2)}) collective-permute-start(f32[2,10,1,256]{3,2,1,0:T(1,128)S(1)} %get-tuple-element.32), channel_id=1, source_target_pairs={{1,0},{2,1},{3,2},{5,4},{6,5},{7,6},{9,8},{10,9},{11,10},{13,12},{... | collective-permute-start | bytes 61448 | tf_op jit(solution)/shard_map/ppermute | solution.py:22
  147.6 3.9 %collective-permute-start.15 = (f32[2,10,1,256]{3,2,1,0:T(1,128)S(1)}, f32[2,10,1,256]{3,2,1,0:T(1,128)S(1)}, u32[]{:S(2)}, u32[]{:S(2)}) collective-permute-start(f32[2,10,1,256]{3,2,1,0:T(1,128)S(1)} %get-tuple-element.33), channel_id=1, source_target_pairs={{0,1},{1,2},{2,3},{4,5},{5,6},{6,7},{8,9},{9,10},{10,11},{12,13},{... | collective-permute-start | bytes 61448 | tf_op jit(solution)/shard_map/ppermute | solution.py:20
  151.4 2.3 %copy-start.4 = (f32[8,128,256]{2,1,0:T(8,128)S(1)}, f32[8,128,256]{2,1,0:T(8,128)}, u32[]{:S(2)}) copy-start(f32[8,128,256]{2,1,0:T(8,128)} %param.6) | copy-start | bytes 3145732
where the time goes:
time: 158 us; the launch traced here: 156 us
  waiting for transfers between devices  63.8 us (40%)
  starting transfers between devices  43.4 us (27%)
  other arithmetic  30.9 us (20%)
  blocking collectives  11.4 us (7%)
  local copies, waits for them, and re-layouts  5.37 us (3%)
    ppermute x8, waiting for transfers between devices, extended(): lax.ppermute(tail, axis, [(i, (i + 1) % count) for i in range(ends)])  36.9 us
    ppermute x8, starting transfers between devices, extended(): lax.ppermute(tail, axis, [(i, (i + 1) % count) for i in range(ends)])  33.1 us
    ppermute x8, waiting for transfers between devices, extended(): lax.ppermute(head, axis, [((i + 1) % count, i) for i in range(ends)])  26.8 us
    sub x4, other arithmetic, lap_inner(): return total - 6.0 * core  20 us
    psum x1, blocking collectives, local(): lax.psum((jnp.sum(state[1], axis=1), jnp.sum(state[3], axis=1)), 'depth')  11.4 us
    ppermute x8, starting transfers between devices, extended(): lax.ppermute(head, axis, [((i + 1) % count, i) for i in range(ends)])  10.3 us
    slice x2, local copies, waits for them, and re-layouts, lap_inner(): total = total + jnp.concatenate([core[..., 1:], zero_col], axis=-1)  5.03 us
  transfers between devices with their start and end apart: 16, of which 10 were waited for; matrix products, arithmetic and copies ran while one was open for 4% of the time, Pallas kernels for 0%

commit v1 on v0

v1 whole, which is shorter than its diff:
```python
import functools
import math

import jax
import jax.numpy as jnp
from jax import lax
from jax.experimental import pallas as pl
from jax.experimental.pallas import tpu as pltpu
from jax.sharding import PartitionSpec as P

MESH = pl.DeviceIdType.MESH
PAD = 16
CH = 24
BC = 32


def growth(labels):
    return jnp.where(
        labels == 0, 0.6, jnp.where(labels == 1, 1.0, jnp.where(labels == 2, 1.7, 0.8))
    ).astype(jnp.float32)


def slopes(p, s, grow):
    shell = 1.0 - p * p
    return grow * (1.0 - 3.0 * p * p) + 4.0 * p * shell * s, -shell * shell


def tiles(block, count):
    return jnp.concatenate([block] * count, axis=0)


def fold(value):
    total = value[0:8]
    for k in range(8, value.shape[0], 8):
        total = total + value[k : k + 8]
    return total


def lanes(value):
    cols = value.shape[1]
    lane = lax.broadcasted_iota(jnp.int32, value.shape, 1)
    left = jnp.where(lane == 0, 0.0, pltpu.roll(value, 1, 1))
    right = jnp.where(lane == cols - 1, 0.0, pltpu.roll(value, cols - 1, 1))
    return left + right


def kernel(
    nt, nd,
    p_hbm, s_hbm, dp_hbm, ds_hbm, lab_hbm, mask_hbm,
    hp_hbm, hs_hbm, change_ref,
    pe, se, dpe, dse, labe, maske, growb,
    c1, a1, wide, solw, hp, hs,
    accs, cross, own_out, up_out, down_out, own_in, up_in, down_in,
    ext, bb, gb, hb,
    local_sem, out_sem, send_sem, recv_sem, own_send, own_recv, up_send, up_recv, down_send, down_recv,
):
    rows, depth, cols = p_hbm.shape
    t = lax.axis_index("tile")
    d = lax.axis_index("depth")
    has_above, has_below = t < nt - 1, t > 0
    has_right, has_left = d < nd - 1, d > 0
    above, below = lax.rem(t + 1, nt), lax.rem(t + nt - 1, nt)
    right, left = lax.rem(d + 1, nd), lax.rem(d + nd - 1, nd)
    end = PAD + depth
    core = slice(PAD, end)
    core_rows = slice(2, 2 + rows)

    local = [
        pltpu.make_async_copy(src, dst, local_sem.at[n])
        for n, (src, dst) in enumerate(
            [
                (p_hbm, pe.at[core_rows, core]),
                (s_hbm, se.at[core_rows, core]),
                (dp_hbm, dpe.at[:, core]),
                (ds_hbm, dse.at[:, core]),
                (lab_hbm, labe.at[rows : 2 * rows]),
                (mask_hbm, maske.at[rows : 2 * rows]),
            ]
        )
    ]
    for copy in local:
        copy.start()

    barrier = pltpu.get_barrier_semaphore()

    def greet(tt, dd):
        pl.semaphore_signal(barrier, inc=1, device_id=(tt, dd), device_id_type=MESH)

    for n in range(1, nd):
        greet(t, lax.rem(d + n, nd))

    @pl.when(has_above)
    def _():
        for n in range(nd):
            greet(above, n)

    @pl.when(has_below)
    def _():
        for n in range(nd):
            greet(below, n)

    beside_count = jnp.where(has_above, 1, 0) + jnp.where(has_below, 1, 0)
    pl.semaphore_wait(barrier, nd - 1 + nd * beside_count)

    number = [0]

    def remote(src, dst, tt, dd):
        n = number[0]
        number[0] = n + 1
        return pltpu.make_async_remote_copy(
            src_ref=src,
            dst_ref=dst,
            send_sem=send_sem.at[n],
            recv_sem=recv_sem.at[n],
            device_id=(tt, dd),
            device_id_type=MESH,
        )

    top, bottom = 2 + rows, 1
    first, last = slice(0, 8), slice(depth - 8, depth)
    after, before = slice(end, end + 8), slice(PAD - 8, PAD)
    pairs = [(p_hbm, pe), (s_hbm, se)]
    to_right = [remote(a.at[:, last], b.at[core_rows, before], t, right) for a, b in pairs]
    to_left = [remote(a.at[:, first], b.at[core_rows, after], t, left) for a, b in pairs]
    for a, b in [(dp_hbm, dpe), (ds_hbm, dse)]:
        to_right.append(remote(a.at[:, last], b.at[:, before], t, right))
        to_left.append(remote(a.at[:, first], b.at[:, after], t, left))
    diagonals = []
    for tt, going_t, coming_t, src_row, dst_row in [
        (above, has_above, has_below, rows - 1, bottom),
        (below, has_below, has_above, 0, top),
    ]:
        for dd, going_d, coming_d, src_k, dst_k in [
            (right, has_right, has_left, last, before),
            (left, has_left, has_right, first, after),
        ]:
            copies = [
                remote(a.at[pl.ds(src_row, 1), src_k], b.at[pl.ds(dst_row, 1), dst_k], tt, dd)
                for a, b in pairs
            ]
            diagonals.append((going_t & going_d, coming_t & coming_d, copies, dst_row, dst_k))
    up_near = [remote(lab_hbm, labe.at[0:rows], above, d), remote(mask_hbm, maske.at[0:rows], above, d)]
    down_near = [
        remote(lab_hbm, labe.at[2 * rows : 3 * rows], below, d),
        remote(mask_hbm, maske.at[2 * rows : 3 * rows], below, d),
    ]
    for a, b in pairs:
        up_near.append(remote(a.at[pl.ds(rows - 1, 1)], b.at[pl.ds(1, 1), core], above, d))
        down_near.append(remote(a.at[pl.ds(0, 1)], b.at[pl.ds(top, 1), core], below, d))
    up_far = [remote(a.at[pl.ds(rows - 2, 1)], b.at[pl.ds(0, 1), core], above, d) for a, b in pairs]
    down_far = [remote(a.at[pl.ds(1, 1)], b.at[pl.ds(top + 1, 1), core], below, d) for a, b in pairs]

    def start(condition, copies):
        @pl.when(condition)
        def _():
            for copy in copies:
                copy.start()

    def arrive(condition, copies):
        @pl.when(condition)
        def _():
            for copy in copies:
                copy.wait_recv()

    def sent(condition, copies):
        @pl.when(condition)
        def _():
            for copy in copies:
                copy.wait_send()

    start(has_above, up_near)
    start(has_below, down_near)
    start(has_right, to_right)
    start(has_left, to_left)
    for going, coming, copies, _, _ in diagonals:
        start(going, copies)
    start(has_above, up_far)
    start(has_below, down_far)

    row_zero = jnp.zeros((depth, cols), jnp.float32)
    tile_zero = jnp.zeros((8, cols), jnp.float32)
    label_zero = jnp.zeros((rows, cols), jnp.int32)

    def no_row(condition, near, far, label_at):
        @pl.when(jnp.logical_not(condition))
        def _():
            for b in (pe, se):
                b[near, core] = row_zero
                b[far, core] = row_zero
            labe[label_at : label_at + rows] = label_zero
            maske[label_at : label_at + rows] = label_zero

    no_row(has_below, 1, 0, 0)
    no_row(has_above, top, top + 1, 2 * rows)

    def no_side(condition, span):
        @pl.when(jnp.logical_not(condition))
        def _():
            for r in range(rows):
                pe[2 + r, span] = tile_zero
                se[2 + r, span] = tile_zero
                dpe[r, span] = tile_zero
                dse[r, span] = tile_zero

    no_side(has_left, before)
    no_side(has_right, after)
    for _, coming, _, dst_row, dst_k in diagonals:

        @pl.when(jnp.logical_not(coming))
        def _():
            pe[dst_row, dst_k] = tile_zero
            se[dst_row, dst_k] = tile_zero

    for copy in local:
        copy.wait()

    def set_growth(j):
        row = labe[rows - 1 + j : rows + j]
        growb[j] = jnp.broadcast_to(growth(row), (8, cols))

    for j in range(1, rows + 1):
        set_growth(j)

    sub = lax.broadcasted_iota(jnp.int32, (CH, cols), 0)
    low_end = jnp.where(d == 0, PAD, -1)
    high_end = jnp.where(d == nd - 1, end - 1, -1)

    def spread(ref, r, k0):
        block = ref[r, pl.ds(pl.multiple_of(k0 - 8, 8), CH + 16), :]
        size = CH + 16
        beside = pltpu.roll(block, 1, 0) + pltpu.roll(block, size - 1, 0)
        center = block[8 : 8 + CH]
        return center, beside[8 : 8 + CH] + lanes(center) - 6.0 * center

    def at(ref, r, k0):
        return ref[r, pl.ds(pl.multiple_of(k0, 8), CH), :]

    def base_next(i, k0, grow):
        p, lap_p = spread(pe, i, k0)
        s, lap_s = spread(se, i, k0)
        lap_p = lap_p + at(pe, i - 1, k0) + at(pe, i + 1, k0)
        lap_s = lap_s + at(se, i - 1, k0) + at(se, i + 1, k0)
        shell = 1.0 - p * p
        p_next = p + 0.1 * (lap_p + grow * (p - p * p * p) - shell * shell * s)
        s_next = s + 0.1 * lap_s + 0.5 * (p_next - p)
        return p, s, p_next, s_next

    def save_slopes(i, k0, slope_p, slope_s, at_end):
        span = pl.ds(pl.multiple_of(k0, 8), CH)
        c1[i - 1, span, :] = 0.05 * slope_p + 0.025 * slope_s - 0.1 * at_end
        a1[i - 1, span, :] = 0.05 * slope_s - 0.1 * at_end

    def ends_of(k0):
        k = sub + k0
        at_end = jnp.where((k == low_end) | (k == high_end), 1.0, 0.0)
        inside = (k >= PAD) & (k < end)
        return at_end, inside

    chunks = (depth + 16) // CH

    def own_row(i, has_lower, has_upper):
        j = i - 2
        grow = tiles(growb[i - 1], CH // 8)

        def one(n, carry):
            k0 = PAD - 8 + n * CH
            at_end, inside = ends_of(k0)
            p, s, p1, s1 = base_next(i, k0, grow)
            slope_p, slope_s = slopes(p, s, grow)
            span = pl.ds(pl.multiple_of(k0, 8), CH)
            wide[j, span, :] = 0.4 + 0.1 * slope_p
            solw[j, span, :] = 0.1 * slope_s
            next_p, next_s = slopes(p1, s1, grow)
            save_slopes(i, k0, next_p, next_s, at_end)
            dp, lap_dp = spread(dpe, j, k0)
            ds, lap_ds = spread(dse, j, k0)
            if has_lower:
                lap_dp = lap_dp + at(dpe, j - 1, k0)
                lap_ds = lap_ds + at(dse, j - 1, k0)
            if has_upper:
                lap_dp = lap_dp + at(dpe, j + 1, k0)
                lap_ds = lap_ds + at(dse, j + 1, k0)
            dp1 = dp + 0.1 * (lap_dp + slope_p * dp + slope_s * ds)
            ds1 = ds + 0.1 * lap_ds + 0.5 * (dp1 - dp)
            weight = 4.0 + at_end
            blend = 0.1 * s1 + 0.05 * p1
            dblend = 0.1 * ds1 + 0.05 * dp1
            term = s1 + 0.05 * (grow * (p1 - p1 * p1 * p1) + next_s * s1) - weight * blend
            dterm = ds1 + 0.05 * (next_p * dp1 + next_s * ds1) - weight * dblend
            parts = (term, blend, dterm, dblend)
            return tuple(c + fold(jnp.where(inside, v, 0.0)) for c, v in zip(carry, parts))

        zero = jnp.zeros((8, cols), jnp.float32)
        sums = lax.fori_loop(0, chunks, one, (zero, zero, zero, zero))
        for q in range(4):
            accs[q, j] = sums[q]

    def halo_row(i, j, slot):
        grow = tiles(growb[i - 1], CH // 8)

        def one(n, carry):
            k0 = PAD - 8 + n * CH
            at_end, inside = ends_of(k0)
            _, _, p1, s1 = base_next(i, k0, grow)
            next_p, next_s = slopes(p1, s1, grow)
            save_slopes(i, k0, next_p, next_s, at_end)
            dp, ds = at(dpe, j, k0), at(dse, j, k0)
            add_p = 0.1 * dp
            add_s = 0.1 * ds + 0.05 * dp
            dblend = 0.1 * add_s + 0.05 * add_p
            dterm = add_s + 0.05 * (next_p * add_p + next_s * add_s) - (4.0 + at_end) * dblend
            return tuple(
                c + fold(jnp.where(inside, v, 0.0)) for c, v in zip(carry, (dterm, dblend))
            )

        zero = jnp.zeros((8, cols), jnp.float32)
        sums = lax.fori_loop(0, chunks, one, (zero, zero))
        cross[slot] = sums[0]
        cross[slot + 1] = sums[1]

    def no_halo_row(i, slot):
        c1[i - 1] = jnp.zeros((end + PAD, cols), jnp.float32)
        a1[i - 1] = jnp.zeros((end + PAD, cols), jnp.float32)
        cross[slot] = tile_zero
        cross[slot + 1] = tile_zero

    arrive(has_left, to_right)
    arrive(has_right, to_left)

    def middle(i, carry):
        own_row(i, True, True)
        return carry

    lax.fori_loop(3, rows + 1, middle, 0)
    for _, coming, copies, _, _ in diagonals:
        arrive(coming, copies)
    arrive(has_below, up_near)
    arrive(has_above, down_near)
    set_growth(0)
    set_growth(rows + 1)
    own_row(2, False, True)
    own_row(rows + 1, True, False)

    arrive(has_below, up_far)
    arrive(has_above, down_far)

    @pl.when(has_below)
    def _():
        halo_row(1, 0, 0)

    @pl.when(jnp.logical_not(has_below))
    def _():
        no_halo_row(1, 0)

    @pl.when(has_above)
    def _():
        halo_row(rows + 2, rows - 1, 2)

    @pl.when(jnp.logical_not(has_above))
    def _():
        no_halo_row(rows + 2, 2)

    place = lax.broadcasted_iota(jnp.int32, (rows, cols), 0)

    def beside_rows(x):
        return jnp.where(place == 0, 0.0, pltpu.roll(x, 1, 0)) + jnp.where(
            place == rows - 1, 0.0, pltpu.roll(x, rows - 1, 0)
        )

    term, blend, dterm, dblend = [jnp.sum(accs[q], axis=1) for q in range(4)]
    x_low, q_low, x_high, q_high = [jnp.sum(cross[q], axis=0, keepdims=True) for q in range(4)]
    own_s = term + lanes(blend) + beside_rows(blend)
    own_d = dterm + lanes(dblend) + beside_rows(dblend)
    own_d = own_d + jnp.where(place == 0, q_low, 0.0) + jnp.where(place == rows - 1, q_high, 0.0)
    low_d = dblend[0:1] + x_low + lanes(q_low)
    high_d = dblend[rows - 1 : rows] + x_high + lanes(q_high)
    line = jnp.zeros((1, cols), jnp.float32)
    own_out[0:rows] = own_s
    own_out[rows : 2 * rows] = own_d
    tail = 2 * rows
    halo = [line, blend[0:1], blend[rows - 1 : rows], line, q_low, low_d, high_d, q_high]
    for n, value in enumerate(halo):
        own_out[tail + n : tail + n + 1] = value
    up_out[0:2] = own_s[rows - 2 : rows]
    up_out[2:3] = halo[2]
    up_out[3:4] = line
    up_out[4:6] = own_d[rows - 2 : rows]
    up_out[6:7] = high_d
    up_out[7:8] = q_high
    down_out[0:1] = line
    down_out[1:2] = halo[1]
    down_out[2:4] = own_s[0:2]
    down_out[4:5] = q_low
    down_out[5:6] = low_d
    down_out[6:8] = own_d[0:2]

    def message(src, inbox, sends, receives, n, slot, tt, dd):
        return pltpu.make_async_remote_copy(
            src_ref=src,
            dst_ref=inbox.at[slot],
            send_sem=sends.at[n],
            recv_sem=receives.at[slot],
            device_id=(tt, dd),
            device_id_type=MESH,
        )

    own_messages = [
        message(own_out, own_in, own_send, own_recv, n - 1, d, t, lax.rem(d + n, nd))
        for n in range(1, nd)
    ]
    up_messages = [message(up_out, up_in, up_send, up_recv, n, d, above, n) for n in range(nd)]
    down_messages = [
        message(down_out, down_in, down_send, down_recv, n, d, below, n) for n in range(nd)
    ]
    start(has_above, up_messages)
    start(has_below, down_messages)
    for copy in own_messages:
        copy.start()
    own_in[d] = own_out[...]

    @pl.when(jnp.logical_not(has_below))
    def _():
        for n in range(nd):
            up_in[n] = tile_zero

    @pl.when(jnp.logical_not(has_above))
    def _():
        for n in range(nd):
            down_in[n] = tile_zero

    ext[...] = jnp.zeros_like(ext)
    for n in range(1, nd):
        slot = lax.rem(d + n, nd)
        message(own_out, own_in, own_send, own_recv, n - 1, slot, t, slot).wait_recv()

    @pl.when(has_below)
    def _():
        for n in range(nd):
            message(up_out, up_in, up_send, up_recv, n, n, above, n).wait_recv()

    @pl.when(has_above)
    def _():
        for n in range(nd):
            message(down_out, down_in, down_send, down_recv, n, n, below, n).wait_recv()

    total, low, high = own_in[0], up_in[0], down_in[0]
    for n in range(1, nd):
        total, low, high = total + own_in[n], low + up_in[n], high + down_in[n]
    for q in range(2):
        ext[q, 0:2] = total[tail + 4 * q : tail + 4 * q + 2] + low[4 * q : 4 * q + 2]
        ext[q, 2 : 2 + rows] = total[q * rows : (q + 1) * rows]
        ext[q, 2:4] += low[4 * q + 2 : 4 * q + 4]
        ext[q, rows : rows + 2] += high[4 * q : 4 * q + 2]
        ext[q, rows + 2 : rows + 4] = (
            total[tail + 4 * q + 2 : tail + 4 * q + 4] + high[4 * q + 2 : 4 * q + 4]
        )
    root = math.sqrt(depth * nd)
    high_rows = ext.shape[1]
    bright = jnp.exp(-ext[0] / root)
    change = -bright * ext[1] / root
    mask = maske[rows - 2 : rows - 2 + high_rows].astype(jnp.float32)
    where = lax.broadcasted_iota(jnp.int32, (high_rows, cols), 0)
    valid = jnp.where(has_below, 0, 2)
    valid_end = jnp.where(has_above, rows + 4, rows + 2)
    inside_rows = (where >= valid) & (where < valid_end)
    back = jnp.where(inside_rows, -bright * mask * change, 0.0)
    change_ref[...] = change[2 : 2 + rows]
    flat = pltpu.roll(back, 1, 0) + pltpu.roll(back, high_rows - 1, 0) + lanes(back) - 4.0 * back
    flat = jnp.where(inside_rows, flat, 0.0)
    g = 0.5 * back + 0.1 * flat
    h = back + 0.1 * flat
    for j in range(rows + 2):
        bb[j] = jnp.broadcast_to(back[j + 1 : j + 2], (8, cols))
        gb[j] = jnp.broadcast_to(g[j + 1 : j + 2], (8, cols))
        hb[j] = jnp.broadcast_to(h[j + 1 : j + 2], (8, cols))

    def carry_row(j, carry):
        b, gg, hh = [tiles(x[j], CH // 8) for x in (bb, gb, hb)]
        for n in range(chunks):
            span = slice(PAD - 8 + n * CH, PAD - 8 + (n + 1) * CH)
            c1[j, span] = gg + c1[j, span] * b
            a1[j, span] = hh + a1[j, span] * b
        return carry

    lax.fori_loop(0, rows + 2, carry_row, 0)

    def no_depth(condition, span):
        @pl.when(jnp.logical_not(condition))
        def _():
            for j in range(rows + 2):
                c1[j, span] = tile_zero
                a1[j, span] = tile_zero

    no_depth(has_left, before)
    no_depth(has_right, after)

    def near(ref, j, k0):
        size = BC + 16
        block = ref[j, k0 - 8 : k0 - 8 + size]
        beside = pltpu.roll(block, 1, 0) + pltpu.roll(block, size - 1, 0)
        center = block[8 : 8 + BC]
        span = slice(k0, k0 + BC)
        return center, beside[8 : 8 + BC] + lanes(center) + ref[j - 1, span] + ref[j + 1, span]

    def out_copies(j):
        return [
            pltpu.make_async_copy(hp.at[j], hp_hbm.at[j], out_sem.at[0, j]),
            pltpu.make_async_copy(hs.at[j], hs_hbm.at[j], out_sem.at[1, j]),
        ]

    def finish(j, carry):
        for n in range(depth // BC):
            k0 = PAD + n * BC
            c, near_c = near(c1, j + 1, k0)
            a, near_a = near(a1, j + 1, k0)
            span = slice(k0, k0 + BC)
            dst = slice(n * BC, (n + 1) * BC)
            hp[j, dst] = c * wide[j, span] + 0.1 * near_c - 0.5 * a
            hs[j, dst] = 0.4 * a + 0.1 * near_a + solw[j, span] * c
        for copy in out_copies(j):
            copy.start()
        return carry

    lax.fori_loop(0, rows, finish, 0)
    for copy in own_messages:
        copy.wait_send()
    sent(has_above, up_messages + up_near + up_far)
    sent(has_below, down_messages + down_near + down_far)
    sent(has_right, to_right)
    sent(has_left, to_left)
    for going, coming, copies, _, _ in diagonals:
        sent(going, copies)
    for j in range(rows):
        for copy in out_copies(j):
            copy.wait()


def local(nt, nd, phase, solute, dphase, dsolute, labels, pixel_mask):
    rows, depth, cols = phase.shape
    f32, i32 = jnp.float32, jnp.int32
    length = depth + 2 * PAD
    dma = pltpu.SemaphoreType.DMA
    any_space = pl.BlockSpec(memory_space=pl.ANY)
    vmem = pl.BlockSpec(memory_space=pltpu.VMEM)
    field = jax.ShapeDtypeStruct((rows, depth, cols), f32)
    return pl.pallas_call(
        functools.partial(kernel, nt, nd),
        out_shape=(field, field, jax.ShapeDtypeStruct((rows, cols), f32)),
        in_specs=[any_space] * 6,
        out_specs=(any_space, any_space, vmem),
        scratch_shapes=[
            pltpu.VMEM((rows + 4, length, cols), f32),
            pltpu.VMEM((rows + 4, length, cols), f32),
            pltpu.VMEM((rows, length, cols), f32),
            pltpu.VMEM((rows, length, cols), f32),
            pltpu.VMEM((3 * rows, cols), i32),
            pltpu.VMEM((3 * rows, cols), i32),
            pltpu.VMEM((rows + 2, 8, cols), f32),
            pltpu.VMEM((rows + 2, length, cols), f32),
            pltpu.VMEM((rows + 2, length, cols), f32),
            pltpu.VMEM((rows, length, cols), f32),
            pltpu.VMEM((rows, length, cols), f32),
            pltpu.VMEM((rows, depth, cols), f32),
            pltpu.VMEM((rows, depth, cols), f32),
            pltpu.VMEM((4, rows, 8, cols), f32),
            pltpu.VMEM((4, 8, cols), f32),
            pltpu.VMEM((2 * rows + 8, cols), f32),
            pltpu.VMEM((8, cols), f32),
            pltpu.VMEM((8, cols), f32),
            pltpu.VMEM((nd, 2 * rows + 8, cols), f32),
            pltpu.VMEM((nd, 8, cols), f32),
            pltpu.VMEM((nd, 8, cols), f32),
            pltpu.VMEM((2, rows + 8, cols), f32),
            pltpu.VMEM((rows + 2, 8, cols), f32),
            pltpu.VMEM((rows + 2, 8, cols), f32),
            pltpu.VMEM((rows + 2, 8, cols), f32),
            dma((6,)),
            dma((2, rows)),
            dma((28,)),
            dma((28,)),
            dma((nd - 1,)),
            dma((nd,)),
            dma((nd,)),
            dma((nd,)),
            dma((nd,)),
            dma((nd,)),
        ],
        compiler_params=pltpu.CompilerParams(
            collective_id=0, has_side_effects=True, vmem_limit_bytes=48 * 1024 * 1024
        ),
    )(phase, solute, dphase, dsolute, labels, pixel_mask)


def solution(mesh):
    field, plane = P("tile", "depth", None), P("tile", None)
    return jax.shard_map(
        functools.partial(local, mesh.shape["tile"], mesh.shape["depth"]),
        mesh=mesh,
        in_specs=(field, field, field, field, plane, plane),
        out_specs=(field, field, plane),
        check_vma=False,
    )
```

time: 158 us -> 49.6 us (0.31); the launches traced: 156 us -> 49.2 us
  waiting for transfers between devices: 63.8 us -> 0 us
  starting transfers between devices: 43.4 us -> 0 us
  Pallas kernels: 0 us -> 41 us
  other arithmetic: 30.9 us -> 0 us
  blocking collectives: 11.4 us -> 0 us
  local copies, waits for them, and re-layouts: 5.37 us -> 7.6 us
    ppermute x16 -> x0, waiting for transfers between devices: 63.8 us -> none  [the longest x8 36.9 us: extended(): lax.ppermute(tail, axis, [(i, (i + 1) % count) for i in range(ends)])]
    ppermute x16 -> x0, starting transfers between devices: 43.4 us -> none  [the longest x8 33.1 us: extended(): lax.ppermute(tail, axis, [(i, (i + 1) % count) for i in range(ends)])]
    pallas_call x0 -> x1, Pallas kernels: none -> 41 us  [local(): pl.pallas_call(functools.partial(kernel, nt, nd), out_shape=(field, field...]
    sub x4 -> x0, other arithmetic: 20 us -> none  [lap_inner(): return total - 6.0 * core]
    psum x1 -> x0, blocking collectives: 11.4 us -> none  [local(): lax.psum((jnp.sum(state[1], axis=1), jnp.sum(state[3], axis=1)), 'depth')]
    unnamed x14 -> x13, local copies, waits for them, and re-layouts: 0.04 us -> 7.6 us
    another operation x7 -> x0, other arithmetic: 5.64 us -> none  [the longest x1 2.45 us: local(): state = jnp.stack([phase, solute, dphase, dsolute])]
    slice x4 -> x0, local copies, waits for them, and re-layouts: 5.18 us -> none  [the longest x2 5.03 us: lap_inner(): total = total + jnp.concatenate([core[..., 1:], zero_col], axis=-1)]
  transfers between devices with their start and end apart: 16 -> 0, of which waited for: 10 -> 0; matrix products, arithmetic and copies ran while one was open for 4% -> 0% of each run, Pallas kernels for 0% -> 0%
where the time goes in v1:
time: 49.6 us; the launch traced here: 49.2 us
  Pallas kernels  41 us (83%)
  local copies, waits for them, and re-layouts  7.6 us (15%)
  between operations  0.65 us (1%)
    pallas_call x1, Pallas kernels, local(): pl.pallas_call(functools.partial(kernel, nt, nd), out_shape=(field, field...  41 us
    unnamed x13, local copies, waits for them, and re-layouts  7.6 us

profile of v1, /device:TPU:0, one launch (start us, length us, event | category | flops | bytes accessed | tf_op | source)
XLA Modules:
  0.0 49.2 jit_solution(7323186282791883630)
XLA Ops:
  0.6 0.0 copy-start
  0.6 1.2 %copy-done = f32[8,128,256]{2,1,0:T(8,128)S(1)} copy-done((f32[8,128,256]{2,1,0:T(8,128)S(1)}, f32[8,128,256]{2,1,0:T(8,128)}, u32[]{:S(2)}) %copy-start) | copy-done | bytes 1048600
  1.9 0.0 copy-start.1
  1.9 1.2 %copy-done.1 = f32[8,128,256]{2,1,0:T(8,128)S(1)} copy-done((f32[8,128,256]{2,1,0:T(8,128)S(1)}, f32[8,128,256]{2,1,0:T(8,128)}, u32[]{:S(2)}) %copy-start.1) | copy-done | bytes 1048600
  3.1 0.0 copy-start.2
  3.1 1.2 %copy-done.2 = f32[8,128,256]{2,1,0:T(8,128)S(1)} copy-done((f32[8,128,256]{2,1,0:T(8,128)S(1)}, f32[8,128,256]{2,1,0:T(8,128)}, u32[]{:S(2)}) %copy-start.2) | copy-done | bytes 1048600
  4.3 0.0 copy-start.3
  4.3 0.7 %copy-done.3 = s32[8,256]{1,0:T(8,128)S(1)} copy-done((s32[8,256]{1,0:T(8,128)S(1)}, s32[8,256]{1,0:T(8,128)}, u32[]{:S(2)}) %copy-start.3) | copy-done | bytes 8216
  5.0 0.0 copy-start.4
  5.0 0.7 %copy-done.4 = s32[8,256]{1,0:T(8,128)S(1)} copy-done((s32[8,256]{1,0:T(8,128)S(1)}, s32[8,256]{1,0:T(8,128)}, u32[]{:S(2)}) %copy-start.4) | copy-done | bytes 8216
  5.7 41.0 %shard_map.85 = (f32[8,128,256]{2,1,0:T(8,128)S(1)}, f32[8,128,256]{2,1,0:T(8,128)S(1)}, f32[8,256]{1,0:T(8,128)S(1)}) custom-call(f32[8,128,256]{2,1,0:T(8,128)S(1)} %copy-done, f32[8,128,256]{2,1,0:T(8,128)S(1)} %copy-done.1, f32[8,128,256]{2,1,0:T(8,128)S(1)} %copy-done.2, f32[8,128,256]{2,1,0:T(8,128)} %ds_hbm.1, s32[8,256]{1,0:T(8,128)S(1)} %copy-done.3, ...), custom_call_target="tpu_custom_call" | custom-call | tf_op jit(solution)/shard_map/pallas_call | solution.py:546
  46.7 1.0 %copy.12 = f32[8,128,256]{2,1,0:T(8,128)} copy(f32[8,128,256]{2,1,0:T(8,128)S(1)} %get-tuple-element.6) | data formatting | bytes 2097152
  47.7 1.0 %copy.13 = f32[8,128,256]{2,1,0:T(8,128)} copy(f32[8,128,256]{2,1,0:T(8,128)S(1)} %get-tuple-element.7) | data formatting | bytes 2097152
  48.6 0.6 %copy.14 = f32[8,256]{1,0:T(8,128)} copy(f32[8,256]{1,0:T(8,128)S(1)} %get-tuple-element.8) | data formatting | bytes 16384
Async XLA Ops:
  0.6 1.2 %copy-start = (f32[8,128,256]{2,1,0:T(8,128)S(1)}, f32[8,128,256]{2,1,0:T(8,128)}, u32[]{:S(2)}) copy-start(f32[8,128,256]{2,1,0:T(8,128)} %p_hbm.1) | copy-start | bytes 3145732
  1.9 1.2 %copy-start.1 = (f32[8,128,256]{2,1,0:T(8,128)S(1)}, f32[8,128,256]{2,1,0:T(8,128)}, u32[]{:S(2)}) copy-start(f32[8,128,256]{2,1,0:T(8,128)} %s_hbm.1) | copy-start | bytes 3145732
  3.1 1.2 %copy-start.2 = (f32[8,128,256]{2,1,0:T(8,128)S(1)}, f32[8,128,256]{2,1,0:T(8,128)}, u32[]{:S(2)}) copy-start(f32[8,128,256]{2,1,0:T(8,128)} %dp_hbm.1) | copy-start | bytes 3145732
  4.3 0.7 %copy-start.3 = (s32[8,256]{1,0:T(8,128)S(1)}, s32[8,256]{1,0:T(8,128)}, u32[]{:S(2)}) copy-start(s32[8,256]{1,0:T(8,128)} %lab_hbm.1) | copy-start | bytes 24580
  5.0 0.7 %copy-start.4 = (s32[8,256]{1,0:T(8,128)S(1)}, s32[8,256]{1,0:T(8,128)}, u32[]{:S(2)}) copy-start(s32[8,256]{1,0:T(8,128)} %mask_hbm.1) | copy-start | bytes 24580

commit v2 on v1

--- a/solution.py
+++ b/solution.py
@@ -586,7 +586,7 @@
             dma((nd,)),
         ],
         compiler_params=pltpu.CompilerParams(
-            collective_id=0, has_side_effects=True, vmem_limit_bytes=48 * 1024 * 1024
+            collective_id=0, has_side_effects=True, vmem_limit_bytes=63 * 1024 * 1024
         ),
     )(phase, solute, dphase, dsolute, labels, pixel_mask)
 

time: 49.6 us -> 44.2 us (0.89)
  local copies, waits for them, and re-layouts: 7.6 us -> 3.93 us
  Pallas kernels: 41 us -> 39.5 us
    unnamed x13 -> x7, local copies, waits for them, and re-layouts: 7.6 us -> 3.93 us
    pallas_call x1, Pallas kernels: 41 us -> 39.5 us  [local(): pl.pallas_call(functools.partial(kernel, nt, nd), out_shape=(field, field...]
where the time goes in v2:
time: 44.2 us; the launch traced here: 44.1 us
  Pallas kernels  39.5 us (89%)
  local copies, waits for them, and re-layouts  3.93 us (9%)
  between operations  0.65 us (1%)
    pallas_call x1, Pallas kernels, local(): pl.pallas_call(functools.partial(kernel, nt, nd), out_shape=(field, field...  39.5 us
    unnamed x7, local copies, waits for them, and re-layouts  3.93 us

profile of v2, /device:TPU:0, one launch (start us, length us, event | category | flops | bytes accessed | tf_op | source)
XLA Modules:
  0.0 44.1 jit_solution(8808762123674825670)
XLA Ops:
  0.6 39.5 %shard_map.85 = (f32[8,128,256]{2,1,0:T(8,128)}, f32[8,128,256]{2,1,0:T(8,128)}, f32[8,256]{1,0:T(8,128)}) custom-call(f32[8,128,256]{2,1,0:T(8,128)} %p_hbm.1, f32[8,128,256]{2,1,0:T(8,128)} %s_hbm.1, f32[8,128,256]{2,1,0:T(8,128)} %dp_hbm.1, f32[8,128,256]{2,1,0:T(8,128)} %ds_hbm.1, s32[8,256]{1,0:T(8,128)} %lab_hbm.1, s32[8,256]{1,0:T(8,128)} %mask_hbm.1), custom_call_target="tpu_custom_call" | custom-call | tf_op jit(solution)/shard_map/pallas_call | solution.py:546
  40.1 0.0 copy-start
  40.2 2.4 %copy.12 = f32[8,128,256]{2,1,0:T(8,128)} copy(f32[8,128,256]{2,1,0:T(8,128)} %get-tuple-element.6) | data formatting | bytes 2097152
  42.5 0.0 copy-done
  42.5 0.0 copy-start.1
  42.5 1.0 %copy.13 = f32[8,128,256]{2,1,0:T(8,128)} copy(f32[8,128,256]{2,1,0:T(8,128)S(1)} %copy-done) | data formatting | bytes 2097152
  43.5 0.0 copy-done.1
  43.5 0.6 %copy.14 = f32[8,256]{1,0:T(8,128)} copy(f32[8,256]{1,0:T(8,128)S(1)} %copy-done.1) | data formatting | bytes 16384
Async XLA Ops:
  40.1 2.4 %copy-start = (f32[8,128,256]{2,1,0:T(8,128)S(1)}, f32[8,128,256]{2,1,0:T(8,128)}, u32[]{:S(2)}) copy-start(f32[8,128,256]{2,1,0:T(8,128)} %get-tuple-element.7) | copy-start | bytes 3145732
  42.5 1.0 %copy-start.1 = (f32[8,256]{1,0:T(8,128)S(1)}, f32[8,256]{1,0:T(8,128)}, u32[]{:S(2)}) copy-start(f32[8,256]{1,0:T(8,128)} %get-tuple-element.8) | copy-start | bytes 24580

commit v3 on v2

--- a/solution.py
+++ b/solution.py
@@ -10,7 +10,7 @@
 
 MESH = pl.DeviceIdType.MESH
 PAD = 16
-CH = 24
+CH = 48
 BC = 32
 
 
@@ -174,8 +174,6 @@
     start(has_left, to_left)
     for going, coming, copies, _, _ in diagonals:
         start(going, copies)
-    start(has_above, up_far)
-    start(has_below, down_far)
 
     row_zero = jnp.zeros((depth, cols), jnp.float32)
     tile_zero = jnp.zeros((8, cols), jnp.float32)
@@ -332,6 +330,8 @@
         return carry
 
     lax.fori_loop(3, rows + 1, middle, 0)
+    start(has_above, up_far)
+    start(has_below, down_far)
     for _, coming, copies, _, _ in diagonals:
         arrive(coming, copies)
     arrive(has_below, up_near)

time: 44.2 us -> 43.8 us (level)
    pallas_call x1, Pallas kernels: 39.5 us -> 39.1 us  [local(): pl.pallas_call(functools.partial(kernel, nt, nd), out_shape=(field, field...]
where the time goes in v3:
time: 43.8 us; the launch traced here: 43.6 us
  Pallas kernels  39.1 us (89%)
  local copies, waits for them, and re-layouts  3.93 us (9%)
  between operations  0.65 us (1%)
    pallas_call x1, Pallas kernels, local(): pl.pallas_call(functools.partial(kernel, nt, nd), out_shape=(field, field...  39.1 us
    unnamed x7, local copies, waits for them, and re-layouts  3.93 us

profile of v3, /device:TPU:0, one launch (start us, length us, event | category | flops | bytes accessed | tf_op | source)
XLA Modules:
  0.0 43.6 jit_solution(1500399768659841609)
XLA Ops:
  0.6 39.1 %shard_map.85 = (f32[8,128,256]{2,1,0:T(8,128)}, f32[8,128,256]{2,1,0:T(8,128)}, f32[8,256]{1,0:T(8,128)}) custom-call(f32[8,128,256]{2,1,0:T(8,128)} %p_hbm.1, f32[8,128,256]{2,1,0:T(8,128)} %s_hbm.1, f32[8,128,256]{2,1,0:T(8,128)} %dp_hbm.1, f32[8,128,256]{2,1,0:T(8,128)} %ds_hbm.1, s32[8,256]{1,0:T(8,128)} %lab_hbm.1, s32[8,256]{1,0:T(8,128)} %mask_hbm.1), custom_call_target="tpu_custom_call" | custom-call | tf_op jit(solution)/shard_map/pallas_call | solution.py:546
  39.7 0.0 copy-start
  39.7 2.4 %copy.12 = f32[8,128,256]{2,1,0:T(8,128)} copy(f32[8,128,256]{2,1,0:T(8,128)} %get-tuple-element.6) | data formatting | bytes 2097152
  42.1 0.0 copy-done
  42.1 0.0 copy-start.1
  42.1 1.0 %copy.13 = f32[8,128,256]{2,1,0:T(8,128)} copy(f32[8,128,256]{2,1,0:T(8,128)S(1)} %copy-done) | data formatting | bytes 2097152
  43.0 0.0 copy-done.1
  43.0 0.6 %copy.14 = f32[8,256]{1,0:T(8,128)} copy(f32[8,256]{1,0:T(8,128)S(1)} %copy-done.1) | data formatting | bytes 16384
Async XLA Ops:
  39.7 2.4 %copy-start = (f32[8,128,256]{2,1,0:T(8,128)S(1)}, f32[8,128,256]{2,1,0:T(8,128)}, u32[]{:S(2)}) copy-start(f32[8,128,256]{2,1,0:T(8,128)} %get-tuple-element.7) | copy-start | bytes 3145732
  42.1 1.0 %copy-start.1 = (f32[8,256]{1,0:T(8,128)S(1)}, f32[8,256]{1,0:T(8,128)}, u32[]{:S(2)}) copy-start(f32[8,256]{1,0:T(8,128)} %get-tuple-element.8) | copy-start | bytes 24580

commit v4 on v3

--- a/solution.py
+++ b/solution.py
@@ -464,7 +464,7 @@
     valid_end = jnp.where(has_above, rows + 4, rows + 2)
     inside_rows = (where >= valid) & (where < valid_end)
     back = jnp.where(inside_rows, -bright * mask * change, 0.0)
-    change_ref[...] = change[2 : 2 + rows]
+    change_ref[...] = -change[2 : 2 + rows]
     flat = pltpu.roll(back, 1, 0) + pltpu.roll(back, high_rows - 1, 0) + lanes(back) - 4.0 * back
     flat = jnp.where(inside_rows, flat, 0.0)
     g = 0.5 * back + 0.1 * flat
@@ -515,8 +515,8 @@
             a, near_a = near(a1, j + 1, k0)
             span = slice(k0, k0 + BC)
             dst = slice(n * BC, (n + 1) * BC)
-            hp[j, dst] = c * wide[j, span] + 0.1 * near_c - 0.5 * a
-            hs[j, dst] = 0.4 * a + 0.1 * near_a + solw[j, span] * c
+            hp[j, dst] = 0.5 * a - c * wide[j, span] - 0.1 * near_c
+            hs[j, dst] = -0.4 * a - 0.1 * near_a - solw[j, span] * c
         for copy in out_copies(j):
             copy.start()
         return carry
@@ -543,7 +543,7 @@
     any_space = pl.BlockSpec(memory_space=pl.ANY)
     vmem = pl.BlockSpec(memory_space=pltpu.VMEM)
     field = jax.ShapeDtypeStruct((rows, depth, cols), f32)
-    return pl.pallas_call(
+    negated = pl.pallas_call(
         functools.partial(kernel, nt, nd),
         out_shape=(field, field, jax.ShapeDtypeStruct((rows, cols), f32)),
         in_specs=[any_space] * 6,
@@ -589,6 +589,7 @@
             collective_id=0, has_side_effects=True, vmem_limit_bytes=63 * 1024 * 1024
         ),
     )(phase, solute, dphase, dsolute, labels, pixel_mask)
+    return tuple(-value for value in negated)
 
 
 def solution(mesh):

time: 43.8 us -> 43.9 us (level)
  other arithmetic: 0 us -> 4.06 us
  local copies, waits for them, and re-layouts: 3.93 us -> 0.01 us
    neg x0 -> x3, other arithmetic: none -> 4.06 us  [local(): return tuple((-value for value in negated))]
    unnamed x7 -> x4, local copies, waits for them, and re-layouts: 3.93 us -> 0.01 us
where the time goes in v4:
time: 43.9 us; the launch traced here: 43.8 us
  Pallas kernels  39 us (89%)
  other arithmetic  4.06 us (9%)
  between operations  0.66 us (2%)
    pallas_call x1, Pallas kernels, local(): pl.pallas_call(functools.partial(kernel, nt, nd), out_shape=(field, field...  39 us
    neg x3, other arithmetic, local(): return tuple((-value for value in negated))  4.06 us

profile of v4, /device:TPU:0, one launch (start us, length us, event | category | flops | bytes accessed | tf_op | source)
XLA Modules:
  0.0 43.8 jit_solution(1685307290569787601)
XLA Ops:
  0.6 39.0 %shard_map.85 = (f32[8,128,256]{2,1,0:T(8,128)}, f32[8,128,256]{2,1,0:T(8,128)}, f32[8,256]{1,0:T(8,128)}) custom-call(f32[8,128,256]{2,1,0:T(8,128)} %p_hbm.1, f32[8,128,256]{2,1,0:T(8,128)} %s_hbm.1, f32[8,128,256]{2,1,0:T(8,128)} %dp_hbm.1, f32[8,128,256]{2,1,0:T(8,128)} %ds_hbm.1, s32[8,256]{1,0:T(8,128)} %lab_hbm.1, s32[8,256]{1,0:T(8,128)} %mask_hbm.1), custom_call_target="tpu_custom_call" | custom-call | tf_op jit(solution)/shard_map/pallas_call | solution.py:546
  39.7 0.0 copy-start.1
  39.7 0.0 copy-start
  39.7 2.4 %neg.9 = f32[8,128,256]{2,1,0:T(8,128)} negate(f32[8,128,256]{2,1,0:T(8,128)} %get-tuple-element.6) | non-fusion elementwise | flops 262144 | bytes 2097152 | tf_op jit(solution)/shard_map/neg | solution.py:592
  42.1 0.0 copy-done.1
  42.1 0.6 %neg.11 = f32[8,256]{1,0:T(8,128)} negate(f32[8,256]{1,0:T(8,128)S(1)} %copy-done.1) | non-fusion elementwise | flops 2048 | bytes 16384 | tf_op jit(solution)/shard_map/neg | solution.py:592
  42.7 0.0 copy-done
  42.7 1.1 %neg.10 = f32[8,128,256]{2,1,0:T(8,128)} negate(f32[8,128,256]{2,1,0:T(8,128)S(1)} %copy-done) | non-fusion elementwise | flops 262144 | bytes 2097152 | tf_op jit(solution)/shard_map/neg | solution.py:592
Async XLA Ops:
  39.7 2.4 %copy-start.1 = (f32[8,256]{1,0:T(8,128)S(1)}, f32[8,256]{1,0:T(8,128)}, u32[]{:S(2)}) copy-start(f32[8,256]{1,0:T(8,128)} %get-tuple-element.8) | copy-start | bytes 24580
  39.7 3.0 %copy-start = (f32[8,128,256]{2,1,0:T(8,128)S(1)}, f32[8,128,256]{2,1,0:T(8,128)}, u32[]{:S(2)}) copy-start(f32[8,128,256]{2,1,0:T(8,128)} %get-tuple-element.7) | copy-start | bytes 3145732

commit v5 on v4

--- a/solution.py
+++ b/solution.py
@@ -335,22 +335,23 @@
     for _, coming, copies, _, _ in diagonals:
         arrive(coming, copies)
     arrive(has_below, up_near)
+    set_growth(0)
+    own_row(2, False, True)
     arrive(has_above, down_near)
-    set_growth(0)
     set_growth(rows + 1)
-    own_row(2, False, True)
     own_row(rows + 1, True, False)
 
     arrive(has_below, up_far)
+
+    @pl.when(has_below)
+    def _():
+        halo_row(1, 0, 0)
+
+    @pl.when(jnp.logical_not(has_below))
+    def _():
+        no_halo_row(1, 0)
+
     arrive(has_above, down_far)
-
-    @pl.when(has_below)
-    def _():
-        halo_row(1, 0, 0)
-
-    @pl.when(jnp.logical_not(has_below))
-    def _():
-        no_halo_row(1, 0)
 
     @pl.when(has_above)
     def _():

time: 43.9 us -> 43.9 us (level)
  no operation moved by 1% of the time
where the time goes in v5:
time: 43.9 us; the launch traced here: 43.8 us
  Pallas kernels  39 us (89%)
  other arithmetic  4.06 us (9%)
  between operations  0.66 us (2%)
    pallas_call x1, Pallas kernels, local(): pl.pallas_call(functools.partial(kernel, nt, nd), out_shape=(field, field...  39 us
    neg x3, other arithmetic, local(): return tuple((-value for value in negated))  4.06 us

profile of v5, /device:TPU:0, one launch (start us, length us, event | category | flops | bytes accessed | tf_op | source)
XLA Modules:
  0.0 43.8 jit_solution(1660221024922474653)
XLA Ops:
  0.6 39.0 %shard_map.85 = (f32[8,128,256]{2,1,0:T(8,128)}, f32[8,128,256]{2,1,0:T(8,128)}, f32[8,256]{1,0:T(8,128)}) custom-call(f32[8,128,256]{2,1,0:T(8,128)} %p_hbm.1, f32[8,128,256]{2,1,0:T(8,128)} %s_hbm.1, f32[8,128,256]{2,1,0:T(8,128)} %dp_hbm.1, f32[8,128,256]{2,1,0:T(8,128)} %ds_hbm.1, s32[8,256]{1,0:T(8,128)} %lab_hbm.1, s32[8,256]{1,0:T(8,128)} %mask_hbm.1), custom_call_target="tpu_custom_call" | custom-call | tf_op jit(solution)/shard_map/pallas_call | solution.py:547
  39.7 0.0 copy-start.1
  39.7 0.0 copy-start
  39.7 2.4 %neg.9 = f32[8,128,256]{2,1,0:T(8,128)} negate(f32[8,128,256]{2,1,0:T(8,128)} %get-tuple-element.6) | non-fusion elementwise | flops 262144 | bytes 2097152 | tf_op jit(solution)/shard_map/neg | solution.py:593
  42.1 0.0 copy-done.1
  42.1 0.6 %neg.11 = f32[8,256]{1,0:T(8,128)} negate(f32[8,256]{1,0:T(8,128)S(1)} %copy-done.1) | non-fusion elementwise | flops 2048 | bytes 16384 | tf_op jit(solution)/shard_map/neg | solution.py:593
  42.7 0.0 copy-done
  42.7 1.1 %neg.10 = f32[8,128,256]{2,1,0:T(8,128)} negate(f32[8,128,256]{2,1,0:T(8,128)S(1)} %copy-done) | non-fusion elementwise | flops 262144 | bytes 2097152 | tf_op jit(solution)/shard_map/neg | solution.py:593
Async XLA Ops:
  39.7 2.4 %copy-start.1 = (f32[8,256]{1,0:T(8,128)S(1)}, f32[8,256]{1,0:T(8,128)}, u32[]{:S(2)}) copy-start(f32[8,256]{1,0:T(8,128)} %get-tuple-element.8) | copy-start | bytes 24580
  39.7 3.0 %copy-start = (f32[8,128,256]{2,1,0:T(8,128)S(1)}, f32[8,128,256]{2,1,0:T(8,128)}, u32[]{:S(2)}) copy-start(f32[8,128,256]{2,1,0:T(8,128)} %get-tuple-element.7) | copy-start | bytes 3145732
